TPU v7x, 256 devices: a whole 4x4x8 slice. The times are simulated.
256 devices in a mesh: item: 64 (over z_lo, y, x, core), week: 4 (over z_hi).
Axes of the slice: x: 4, y: 4, z: 8 (z_hi: 4, z_lo: 2; z = z_hi * 2 + z_lo), core: 2. Of those that a mesh axis runs over, the one named last changes fastest.
Arguments:
- counts: int32 [128, 256, 16384], P(None, 'week', 'item'), may hold values from 0 to 7, as said below
- user_factor: float32 [128, 64], replicated, may hold values from 0.3 to 1.5
- item_factor: float32 [16384, 64], P('item'), may hold values from 0.001 to 12, as said below
- week_factor: float32 [256, 64], P('week'), may hold values from 0.001 to 1.5, as said below
Outputs:
- updated_users: float32 [128, 64], replicated
Inputs may be any that keep to these rules, and one draw needn't show every extreme that they name: `counts`: every user has at least one positive count. `item_factor`: positive entries. `week_factor`: positive entries.
All inputs are finite; a program needn't handle non-finite values.
Results may differ from a plain program's by a relative error of at most 0.0003.
Values sent between devices are 32-bit elements; how exact they have to be, the bound alone decides.
A program may use at most 128 MiB of HBM per device.

v0:
```python
import jax
import jax.numpy as jnp
from jax import lax
from jax.sharding import PartitionSpec as P

ITERS = 3


def combine(partials):
    return lax.psum(partials, ("item", "week"))


def per_device(counts, user_factor, item_factor, week_factor):
    rank_width = user_factor.shape[1]
    user_rows = user_factor.shape[0]
    khatri_rao = (week_factor[:, None, :] * item_factor[None, :, :]).reshape(-1, rank_width)
    flat_counts = counts.reshape(user_rows, -1)
    local_items = jnp.sum(item_factor, axis=0)
    local_weeks = jnp.sum(week_factor, axis=0)
    denominator = None
    item_totals = lax.psum(local_items, "item")
    week_totals = lax.psum(local_weeks, "week")
    denominator = item_totals * week_totals
    factor = user_factor
    for iteration in range(ITERS):
        model = jnp.dot(factor, khatri_rao.T, precision=lax.Precision.HIGHEST)
        ratio = flat_counts.astype(jnp.float32) / model
        partial_phi = jnp.dot(ratio, khatri_rao, precision=lax.Precision.HIGHEST)
        summed = combine((partial_phi,))[0]
        factor = factor * summed / denominator[None, :]
    return factor


def solution(mesh):
    placed = (P(None, "week", "item"), P(), P("item", None), P("week", None))
    return jax.shard_map(per_device, mesh=mesh, in_specs=placed, out_specs=P(), check_vma=False)
```

profile of v0, /device:TPU:1, one launch (start us, length us, event | category | flops | bytes accessed | tf_op | source)
XLA Modules:
  0.0 467.0 jit_solution(5044870251818513201)
XLA Ops:
  0.0 0.9 reduce_sum.18
  0.9 141.0 %psum.36 = f32[64]{0:T(128)S(1)} all-reduce(f32[64]{0:T(128)S(1)} %reduce_sum.18), channel_id=1, replica_groups=mesh['item'=64,'week'=4] {'item'}, use_global_device_ids=true, to_apply=%region_2.0 | all-reduce | flops 64 | bytes 512 | tf_op jit(solution)/shard_map/psum | solution.py:21
  142.0 0.8 reduce_sum.19
  142.8 11.2 %psum.37 = f32[64]{0:T(128)S(1)} all-reduce(f32[64]{0:T(128)S(1)} %reduce_sum.19), channel_id=1, replica_groups=mesh['item'=64,'week'=4] {'week'}, use_global_device_ids=true, to_apply=%region_4.0 | all-reduce | flops 64 | bytes 512 | tf_op jit(solution)/shard_map/psum | solution.py:22
  153.9 0.0 copy-start.3
  153.9 1.6 multiply_bitcast_fusion
  155.5 2.3 copy.12
  157.9 0.5 copy-done.3
  158.4 4.1 convert_element_type.8
  162.5 0.0 copy-start.4
  162.5 9.2 %copy.6 = f32[128,64,256]{0,2,1:T(8,128)} copy(f32[128,64,256]{2,1,0:T(8,128)} %convert_element_type.8) | data formatting | bytes 16777216 | tf_op jit(solution)/shard_map/convert_element_type | solution.py:27
  171.7 0.0 copy-done.4
  171.7 0.0 copy-start
  171.7 16.9 %fusion = f32[128,16384]{0,1:T(8,128)S(1)} fusion(f32[128,16384]{0,1:T(8,128)} %bitcast.25, f32[16384,64]{0,1:T(8,128)} %bitcast.19, f32[128,64]{0,1:T(8,128)S(1)} %copy-done.4), kind=kOutput, calls=%fused_computation.1 | convolution fusion | flops 1612709888 | bytes 21004288 | tf_op jit(solution)/shard_map/dot_general | solution.py:26
  188.6 0.0 copy-done
  188.7 5.6 %fusion.1 = f32[128,64]{0,1:T(8,128)S(1)} fusion(f32[128,16384]{0,1:T(8,128)S(1)} %fusion, f32[16384,64]{0,1:T(8,128)S(1)} %bitcast.22), kind=kOutput, calls=%fused_computation.8 | convolution fusion | flops 1610612736 | bytes 12615680 | tf_op jit(solution)/shard_map/dot_general | solution.py:28
  194.2 78.5 %psum.35 = f32[128,64]{0,1:T(8,128)S(1)} all-reduce(f32[128,64]{0,1:T(8,128)S(1)} %fusion.1), channel_id=1, replica_groups=mesh['item'=64,'week'=4] {'item','week'}, use_global_device_ids=true, to_apply=%region_0.0 | all-reduce | flops 8192 | bytes 65536 | tf_op jit(solution)/shard_map/psum | solution.py:10
  272.8 0.0 copy-start.1
  272.8 16.7 %convolution_divide_fusion.1 = f32[128,16384]{0,1:T(8,128)S(1)} fusion(f32[128,16384]{0,1:T(8,128)} %bitcast.26, f32[16384,64]{0,1:T(8,128)} %bitcast.20, f32[128,64]{0,1:T(8,128)S(1)} %copy-done.4, f32[128,64]{0,1:T(8,128)S(1)} %psum.35, f32[64]{0:T(128)S(1)} %mul.34), kind=kOutput, calls=%fused_computation.3 | convolution fusion | flops 1612726272 | bytes 21037312 | tf_op jit(solution)/shard_map/dot_general | solution.py:26
  289.5 0.0 copy-done.1
  289.5 5.6 %fusion.2 = f32[128,64]{0,1:T(8,128)S(1)} fusion(f32[128,16384]{0,1:T(8,128)S(1)} %convolution_divide_fusion.1, f32[16384,64]{0,1:T(8,128)S(1)} %bitcast.23), kind=kOutput, calls=%fused_computation.9 | convolution fusion | flops 1610612736 | bytes 12615680 | tf_op jit(solution)/shard_map/dot_general | solution.py:28
  295.1 74.8 %psum.38 = f32[128,64]{0,1:T(8,128)S(1)} all-reduce(f32[128,64]{0,1:T(8,128)S(1)} %fusion.2), channel_id=1, replica_groups=mesh['item'=64,'week'=4] {'item','week'}, use_global_device_ids=true, to_apply=%region_5.0 | all-reduce | flops 8192 | bytes 65536 | tf_op jit(solution)/shard_map/psum | solution.py:10
  369.8 0.1 multiply_divide_fusion.1
  369.9 0.0 copy-start.2
  369.9 16.7 %convolution_divide_fusion = f32[128,16384]{0,1:T(8,128)S(1)} fusion(f32[128,16384]{0,1:T(8,128)} %bitcast.27, f32[128,64]{0,1:T(8,128)S(1)} %multiply_divide_fusion.1, f32[16384,64]{0,1:T(8,128)} %bitcast.21), kind=kOutput, calls=%fused_computation.2 | convolution fusion | flops 1612709888 | bytes 21004288 | tf_op jit(solution)/shard_map/dot_general | solution.py:26
  386.6 0.0 copy-done.2
  386.6 5.6 %fusion.3 = f32[128,64]{0,1:T(8,128)S(1)} fusion(f32[128,16384]{0,1:T(8,128)S(1)} %convolution_divide_fusion, f32[16384,64]{0,1:T(8,128)S(1)} %bitcast.24), kind=kOutput, calls=%fused_computation.10 | convolution fusion | flops 1610612736 | bytes 12615680 | tf_op jit(solution)/shard_map/dot_general | solution.py:28
  392.2 73.6 %psum.39 = f32[128,64]{0,1:T(8,128)S(1)} all-reduce(f32[128,64]{0,1:T(8,128)S(1)} %fusion.3), channel_id=1, replica_groups=mesh['item'=64,'week'=4] {'item','week'}, use_global_device_ids=true, to_apply=%region_6.0 | all-reduce | flops 8192 | bytes 65536 | tf_op jit(solution)/shard_map/psum | solution.py:10
  465.8 0.7 multiply_divide_fusion
  (1 shorter events, 0.0 us)
Async XLA Ops:
  153.9 4.4 copy-start.3
  162.5 9.2 %copy-start.4 = (f32[128,64]{0,1:T(8,128)S(1)}, f32[128,64]{0,1:T(8,128)}, u32[]{:S(2)}) copy-start(f32[128,64]{0,1:T(8,128)} %param.5) | copy-start | bytes 98308
  171.7 16.9 %copy-start = (f32[64,8,8,256]{3,2,0,1:T(8,128)S(1)}, f32[64,8,8,256]{3,2,0,1:T(8,128)}, u32[]{:S(2)}) copy-start(f32[64,8,8,256]{3,2,0,1:T(8,128)} %copy.12) | copy-start | bytes 12582916
  272.8 16.7 %copy-start.1 = (f32[64,8,8,256]{3,2,0,1:T(8,128)S(1)}, f32[64,8,8,256]{3,2,0,1:T(8,128)}, u32[]{:S(2)}) copy-start(f32[64,8,8,256]{3,2,0,1:T(8,128)} %copy.12) | copy-start | bytes 12582916
  369.9 16.7 %copy-start.2 = (f32[64,8,8,256]{3,2,0,1:T(8,128)S(1)}, f32[64,8,8,256]{3,2,0,1:T(8,128)}, u32[]{:S(2)}) copy-start(f32[64,8,8,256]{3,2,0,1:T(8,128)} %copy.12) | copy-start | bytes 12582916
where the time goes:
time: 474 us; the launch traced here: 467 us
  blocking collectives  379 us (80%)
  matrix products  67 us (14%)
  local copies, waits for them, and re-layouts  12.1 us (3%)
  other arithmetic  8.19 us (2%)
    psum x3, blocking collectives, combine(): return lax.psum(partials, ('item', 'week'))  227 us
    psum x1, blocking collectives, per_device(): item_totals = lax.psum(local_items, 'item')  141 us
    dot_general x3, matrix products, per_device(): model = jnp.dot(factor, khatri_rao.T, precision=lax.Precision.HIGHEST)  50.3 us
    dot_general x3, matrix products, per_device(): partial_phi = jnp.dot(ratio, khatri_rao, precision=lax.Precision.HIGHEST)  16.7 us
    psum x1, blocking collectives, per_device(): week_totals = lax.psum(local_weeks, 'week')  11.2 us

commit v1 on v0

v1 whole, which is shorter than its diff:
```python
import functools

import jax
import jax.numpy as jnp
from jax import lax
from jax.experimental import pallas as pl
from jax.experimental.pallas import tpu as pltpu
from jax.sharding import PartitionSpec as P

MESH = pl.DeviceIdType.MESH
F32, BF16 = jnp.float32, jnp.bfloat16
ITERS = 3
USERS, RANK, WEEKS, ITEMS = 128, 64, 64, 256
HALF, CHUNK, BLOCK = 64, 32, 16
CHUNKS = HALF // CHUNK
PACK = CHUNK // 2
X, Y, Z = 4, 4, 8


def by_distance(offsets, sizes):
    far = lambda o: sum(min(d, n - d) for d, n in zip(o, sizes))
    return sorted(offsets, key=far, reverse=True)


PLANE = by_distance([(dx, dy) for dx in range(X) for dy in range(Y) if dx or dy], (X, Y))
RING = by_distance([(dz,) for dz in range(1, Z)], (Z,))


def rows_of(step, chunk):
    return PACK + 8 if step == 0 and chunk == 0 else PACK


def kernel(
    counts_hbm, user_hbm, item_hbm, week_hbm, out_ref,
    counts, user, items, week, pair_week, model_rhs, phi_rhs, models, factor, phi,
    half_src, half_dst, plane, ring, last_src, last_dst,
    load_sem, count_sem, item_sems, swap_send, swap_recv,
    half_send, half_recv, plane_send, plane_recv, ring_send, ring_recv, last_send, last_recv,
):
    item, z_hi = lax.axis_index("item"), lax.axis_index("week")
    core, flat = lax.rem(item, 2), lax.rem(item // 2, X * Y)
    x, y = lax.rem(flat, X), flat // X
    z = z_hi * 2 + item // (2 * X * Y)
    other = {"item": item + 1 - 2 * core, "week": z_hi}

    def in_plane(dx, dy):
        there = lax.rem(y + dy, Y) * X + lax.rem(x + dx, X)
        return {"item": item + (there - flat) * 2, "week": z_hi}

    def in_ring(dz):
        there = lax.rem(z + dz, Z)
        return {"item": lax.rem(there, 2) * (2 * X * Y) + flat * 2 + core, "week": there // 2}

    plane_peers = [in_plane(*o) for o in PLANE]
    ring_peers = [in_ring(*o) for o in RING]
    barrier = pltpu.get_barrier_semaphore()
    for peer in [other, *plane_peers, *ring_peers]:
        pl.semaphore_signal(barrier, inc=1, device_id=peer, device_id_type=MESH)

    def remote(src, dst, send, recv, peer):
        return pltpu.make_async_remote_copy(
            src_ref=src, dst_ref=dst, send_sem=send, recv_sem=recv, device_id=peer, device_id_type=MESH
        )

    own_first, other_first = core * HALF, (1 - core) * HALF

    loads = [
        pltpu.make_async_copy(src, dst, load_sem.at[i])
        for i, (src, dst) in enumerate(((item_hbm, items.at[0]), (week_hbm, week), (user_hbm, user)))
    ]
    for load in loads:
        load.start()
    first_blocks = []
    for chunk in range(CHUNKS):
        starts = [first + chunk * CHUNK + b * BLOCK for first in (other_first, own_first) for b in range(CHUNK // BLOCK)]
        first_blocks.append([pl.multiple_of(s, BLOCK) for s in starts])
    count_loads = []
    for chunk in range(CHUNKS):
        for b, start in enumerate(first_blocks[chunk]):
            at = pl.ds(start, BLOCK)
            load = pltpu.make_async_copy(counts_hbm.at[at], counts.at[at], count_sem.at[chunk * 4 + b])
            load.start()
            count_loads.append(load)
    for load in loads:
        load.wait()

    lane = lax.broadcasted_iota(jnp.int32, (1, 2 * RANK), 1)
    left = lane < RANK
    low_lanes = jnp.where(left, 0.0, 1.0).astype(F32)

    def build_rhs(which):
        values = items[which]
        high = values.astype(BF16).astype(F32)
        both = jnp.concatenate([high, values - high], axis=1)
        phi_rhs[which] = both.astype(BF16)
        turned = both.T
        high, low = turned[:RANK], turned[RANK:]
        model_rhs[which] = jnp.concatenate([high, high, low, low], axis=0).astype(BF16)

    build_rhs(0)
    weeks = week[...]
    pair_week[...] = jnp.concatenate([weeks, weeks], axis=1)
    share = jnp.sum(items[0], axis=0, keepdims=True) * jnp.sum(weeks, axis=0, keepdims=True)
    share = jnp.broadcast_to(jnp.concatenate([share, share], axis=1), (8, 2 * RANK))

    packed = {}
    for chunk in range(CHUNKS):
        for half, first in enumerate((own_first, other_first)):
            rows = user[pl.ds(pl.multiple_of(first + chunk * CHUNK, CHUNK), CHUNK), :]
            factor[half, chunk] = jnp.concatenate([rows, rows], axis=1)
            if half == 0:
                packed[chunk] = jnp.concatenate([rows[:PACK], rows[PACK:]], axis=1)

    def model(block):
        _, half, chunk, row, which, _ = block
        w = pair_week[...]
        parts = []
        for u in range(BLOCK):
            scaled = factor[half, chunk, row + u : row + u + 1, :] * w
            high = scaled.astype(BF16).astype(F32)
            parts.append((scaled - high * low_lanes).astype(BF16))
        lhs = jnp.concatenate(parts, axis=0)
        return jnp.dot(jnp.concatenate([lhs, lhs], axis=1), model_rhs[which], preferred_element_type=F32)

    def accumulate(block, slot):
        start, half, _, row, which, add = block
        c = counts[pl.ds(start, BLOCK)].reshape(BLOCK * WEEKS, ITEMS).astype(F32)
        ratio = c * pl.reciprocal(models[slot], approx=False)
        high = ratio.astype(BF16)
        low = (ratio - high.astype(F32)).astype(BF16)
        rhs = phi_rhs[which]
        sums = jnp.dot(high, rhs, preferred_element_type=F32) + jnp.dot(low, rhs, preferred_element_type=F32)
        sums = jnp.sum(sums.reshape(BLOCK, WEEKS, 2 * RANK) * pair_week[...][None], axis=1)
        if add:
            sums = sums + phi[half, row : row + BLOCK, :]
        phi[half, row : row + BLOCK, :] = sums

    def pack(half):
        both = phi[half]
        both = both + pltpu.roll(both, RANK, 1)
        return jnp.where(left, both[:PACK], both[PACK:])

    def compute(blocks, before, after):
        before(0)
        models[0] = model(blocks[0])
        for j, block in enumerate(blocks):
            if j + 1 < len(blocks):
                coming = model(blocks[j + 1])
                before(j + 1)
            accumulate(block, j % 2)
            if j + 1 < len(blocks):
                models[(j + 1) % 2] = coming
            after(j)

    def send_half(chunk):
        n = rows_of(0, chunk)
        half_src[chunk, :PACK] = pack(1)
        if n > PACK:
            half_src[chunk, PACK:n] = share
        at = pl.ds(0, n)
        remote(half_src.at[chunk, at], half_dst.at[chunk, at], half_send.at[chunk], half_recv.at[chunk], other).start()

    def wait_bytes(ref, sem):
        pltpu.make_async_copy(ref, ref, sem).wait()

    def send_plane(step, chunk):
        n = rows_of(step, chunk)
        mine = pack(0)
        if step == 0:
            wait_bytes(half_dst.at[chunk, pl.ds(0, n)], half_recv.at[chunk])
            mine = mine + half_dst[chunk, :PACK]
            if n > PACK:
                plane[step, chunk, flat, PACK:n] = share + half_dst[chunk, PACK:n]
        plane[step, chunk, flat, :PACK] = mine
        block = plane.at[step, chunk, flat, pl.ds(0, n)]
        for peer in plane_peers:
            remote(block, block, plane_send.at[step, chunk], plane_recv.at[step, chunk], peer).start()

    def total(ref, step, chunk, n, count):
        parts = [ref[step, chunk, j, :n] for j in range(count)]
        while len(parts) > 1:
            parts = [a + b for a, b in zip(parts[::2], parts[1::2])]
        return parts[0]

    def send_ring(step, chunk):
        n = rows_of(step, chunk)
        wait_bytes(plane.at[step, chunk, pl.ds(0, X * Y - 1), pl.ds(0, n)], plane_recv.at[step, chunk])
        ring[step, chunk, z, :n] = total(plane, step, chunk, n, X * Y)
        block = ring.at[step, chunk, z, pl.ds(0, n)]
        for peer in ring_peers:
            remote(block, block, ring_send.at[step, chunk], ring_recv.at[step, chunk], peer).start()

    denominator = {}

    def update(step, chunk):
        n = rows_of(step, chunk)
        wait_bytes(ring.at[step, chunk, pl.ds(0, Z - 1), pl.ds(0, n)], ring_recv.at[step, chunk])
        sums = total(ring, step, chunk, n, Z)
        if n > PACK:
            denominator[0] = sums[PACK : PACK + 1]
        packed[chunk] = packed[chunk] * sums[:PACK] / denominator[0]
        if step < ITERS - 1:
            turned = pltpu.roll(packed[chunk], RANK, 1)
            factor[0, chunk, :PACK] = jnp.where(left, packed[chunk], turned)
            factor[0, chunk, PACK:] = jnp.where(left, turned, packed[chunk])

    def first(chunk):
        blocks = [
            (start, 1 - b // 2, chunk, (b % 2) * BLOCK, 0, False) for b, start in enumerate(first_blocks[chunk])
        ]

        def after(j):
            if j == 1:
                if chunk == 0:
                    pl.semaphore_wait(barrier, 1 + len(plane_peers) + len(ring_peers))
                    remote(items.at[0], items.at[1], item_sems.at[0], item_sems.at[1], other).start()
                send_half(chunk)

        compute(blocks, lambda j: count_loads[chunk * 4 + j].wait(), after)

    first(0)
    send_plane(0, 0)
    first(1)
    swaps = []
    for chunk in range(CHUNKS):
        theirs = pl.ds(pl.multiple_of(other_first + chunk * CHUNK, CHUNK), CHUNK)
        landing = pl.ds(USERS + chunk * CHUNK, CHUNK)
        swap = remote(counts_hbm.at[theirs], counts.at[landing], swap_send.at[chunk], swap_recv.at[chunk], other)
        swap.start()
        swaps.append(swap)
    send_plane(0, 1)
    wait_bytes(items.at[1], item_sems.at[1])
    build_rhs(1)
    send_ring(0, 0)
    send_ring(0, 1)
    update(0, 0)

    def later(chunk):
        own = pl.multiple_of(own_first + chunk * CHUNK, CHUNK)
        starts = [own, own + BLOCK, USERS + chunk * CHUNK, USERS + chunk * CHUNK + BLOCK]
        blocks = [(start, 0, chunk, (b % 2) * BLOCK, b // 2, b >= 2) for b, start in enumerate(starts)]
        compute(blocks, lambda j: None, lambda j: None)

    for step in range(1, ITERS):
        if step == 1:
            swaps[0].wait_recv()
        later(0)
        send_plane(step, 0)
        update(step - 1, 1)
        if step == 1:
            swaps[1].wait_recv()
        later(1)
        send_plane(step, 1)
        send_ring(step, 0)
        send_ring(step, 1)
        update(step, 0)
        if step == ITERS - 1:
            send_last = []
            for chunk in range(CHUNKS):
                if chunk:
                    update(step, chunk)
                last_src[chunk] = packed[chunk]
                copy = remote(last_src.at[chunk], last_dst.at[chunk], last_send.at[chunk], last_recv.at[chunk], other)
                copy.start()
                send_last.append(copy)

    def write(first, chunk, rows):
        at = first + chunk * CHUNK
        out_ref[pl.ds(pl.multiple_of(at, PACK), PACK), :] = rows[:, :RANK]
        out_ref[pl.ds(pl.multiple_of(at + PACK, PACK), PACK), :] = rows[:, RANK:]

    for chunk in range(CHUNKS):
        write(own_first, chunk, packed[chunk])
    for chunk in range(CHUNKS):
        send_last[chunk].wait_recv()
        write(other_first, chunk, last_dst[chunk])

    wait_bytes(items.at[0], item_sems.at[0])
    for chunk in range(CHUNKS):
        send_last[chunk].wait_send()
        swaps[chunk].wait_send()
        wait_bytes(half_src.at[chunk, pl.ds(0, rows_of(0, chunk))], half_send.at[chunk])
        for step in range(ITERS):
            n = pl.ds(0, rows_of(step, chunk))
            wait_bytes(plane.at[step, chunk, pl.ds(0, X * Y - 1), n], plane_send.at[step, chunk])
            wait_bytes(ring.at[step, chunk, pl.ds(0, Z - 1), n], ring_send.at[step, chunk])


def per_device(counts, user_factor, item_factor, week_factor):
    most = PACK + 8
    dma = pltpu.SemaphoreType.DMA
    return pl.pallas_call(
        kernel,
        out_shape=jax.ShapeDtypeStruct((USERS, RANK), F32),
        in_specs=[pl.BlockSpec(memory_space=pl.ANY)] * 4,
        out_specs=pl.BlockSpec(memory_space=pltpu.VMEM),
        scratch_shapes=[
            pltpu.VMEM((USERS + HALF, WEEKS, ITEMS), jnp.int32),
            pltpu.VMEM((USERS, RANK), F32),
            pltpu.VMEM((2, ITEMS, RANK), F32),
            pltpu.VMEM((WEEKS, RANK), F32),
            pltpu.VMEM((WEEKS, 2 * RANK), F32),
            pltpu.VMEM((2, 4 * RANK, ITEMS), BF16),
            pltpu.VMEM((2, ITEMS, 2 * RANK), BF16),
            pltpu.VMEM((2, BLOCK * WEEKS, ITEMS), F32),
            pltpu.VMEM((2, CHUNKS, CHUNK, 2 * RANK), F32),
            pltpu.VMEM((2, CHUNK, 2 * RANK), F32),
            pltpu.VMEM((CHUNKS, most, 2 * RANK), F32),
            pltpu.VMEM((CHUNKS, most, 2 * RANK), F32),
            pltpu.VMEM((ITERS, CHUNKS, X * Y, most, 2 * RANK), F32),
            pltpu.VMEM((ITERS, CHUNKS, Z, most, 2 * RANK), F32),
            pltpu.VMEM((CHUNKS, PACK, 2 * RANK), F32),
            pltpu.VMEM((CHUNKS, PACK, 2 * RANK), F32),
            dma((3,)), dma((CHUNKS * 4,)), dma((2,)), dma((CHUNKS,)), dma((CHUNKS,)),
            dma((CHUNKS,)), dma((CHUNKS,)), dma((ITERS, CHUNKS)), dma((ITERS, CHUNKS)),
            dma((ITERS, CHUNKS)), dma((ITERS, CHUNKS)), dma((CHUNKS,)), dma((CHUNKS,)),
        ],
        compiler_params=pltpu.CompilerParams(
            collective_id=0, has_side_effects=True, vmem_limit_bytes=40 << 20
        ),
        name="updates",
    )(counts, user_factor, item_factor, week_factor)


def solution(mesh):
    placed = (P(None, "week", "item"), P(), P("item", None), P("week", None))
    return jax.shard_map(per_device, mesh=mesh, in_specs=placed, out_specs=P(), check_vma=False)
```

time: 474 us -> 56.4 us (0.12); the launches traced: 467 us -> 56.1 us
  blocking collectives: 379 us -> 0 us
  matrix products: 67 us -> 0 us
  Pallas kernels: 0 us -> 49.5 us
  other arithmetic: 8.19 us -> 0 us
  local copies, waits for them, and re-layouts: 12.1 us -> 6.62 us
    psum x5 -> x0, blocking collectives: 379 us -> none  [the longest x3 227 us: combine(): return lax.psum(partials, ('item', 'week'))]
    dot_general x6 -> x0, matrix products: 67 us -> none  [the longest x3 50.3 us: per_device(): model = jnp.dot(factor, khatri_rao.T, precision=lax.Precision.HIGHEST)]
    pallas_call x0 -> x1, Pallas kernels: none -> 49.5 us  [per_device(): pl.pallas_call(kernel, out_shape=jax.ShapeDtypeStruct((USERS, RANK), F32)...]
    convert_element_type x1 -> x0, local copies, waits for them, and re-layouts: 9.24 us -> none  [per_device(): ratio = flat_counts.astype(jnp.float32) / model]
    unnamed x10 -> x6, local copies, waits for them, and re-layouts: 0.53 us -> 5.92 us
where the time goes in v1:
time: 56.4 us; the launch traced here: 56.1 us
  Pallas kernels  49.5 us (88%)
  local copies, waits for them, and re-layouts  6.62 us (12%)
    pallas_call x1, Pallas kernels, per_device(): pl.pallas_call(kernel, out_shape=jax.ShapeDtypeStruct((USERS, RANK), F32)...  49.5 us
    unnamed x6, local copies, waits for them, and re-layouts  5.92 us

profile of v1, /device:TPU:1, one launch (start us, length us, event | category | flops | bytes accessed | tf_op | source)
XLA Modules:
  0.0 56.1 jit_solution(1147932381962929746)
XLA Ops:
  0.0 0.8 %copy.5.user_hbm = f32[128,64]{1,0:T(8,128)S(1)} copy(f32[128,64]{0,1:T(8,128)} %param.5) | data formatting | bytes 65536 | tf_op args[1]
  0.9 0.9 %copy.6.item_hbm = f32[256,64]{1,0:T(8,128)S(1)} copy(f32[256,64]{0,1:T(8,128)} %param.6) | data formatting | bytes 131072 | tf_op args[2]
  1.8 0.0 copy-start
  1.8 3.4 %copy-done = s32[128,64,256]{2,1,0:T(8,128)S(1)} copy-done((s32[128,64,256]{2,1,0:T(8,128)S(1)}, s32[128,64,256]{2,1,0:T(8,128)}, u32[]{:S(2)}) %copy-start) | copy-done | bytes 8388632
  5.2 0.0 copy-start.1
  5.2 0.8 %copy-done.1 = f32[64,64]{1,0:T(8,128)S(1)} copy-done((f32[64,64]{1,0:T(8,128)S(1)}, f32[64,64]{1,0:T(8,128)}, u32[]{:S(2)}) %copy-start.1) | copy-done | bytes 16408
  5.9 49.5 %updates.1 = f32[128,64]{1,0:T(8,128)S(1)} custom-call(s32[128,64,256]{2,1,0:T(8,128)S(1)} %copy-done, f32[128,64]{1,0:T(8,128)S(1)} %copy.5.user_hbm, f32[256,64]{1,0:T(8,128)S(1)} %copy.6.item_hbm, f32[64,64]{1,0:T(8,128)S(1)} %copy-done.1), custom_call_target="tpu_custom_call" | custom-call | tf_op jit(solution)/shard_map/updates/pallas_call | solution.py:292
  55.4 0.7 %copy.7 = f32[128,64]{0,1:T(8,128)} copy(f32[128,64]{1,0:T(8,128)S(1)} %updates.1) | data formatting | bytes 65536 | tf_op jit(solution)/shard_map/updates/pallas_call | solution.py:292
Async XLA Ops:
  1.8 3.4 %copy-start = (s32[128,64,256]{2,1,0:T(8,128)S(1)}, s32[128,64,256]{2,1,0:T(8,128)}, u32[]{:S(2)}) copy-start(s32[128,64,256]{2,1,0:T(8,128)} %counts_hbm.1) | copy-start | bytes 25165828
  5.2 0.8 %copy-start.1 = (f32[64,64]{1,0:T(8,128)S(1)}, f32[64,64]{1,0:T(8,128)}, u32[]{:S(2)}) copy-start(f32[64,64]{1,0:T(8,128)} %week_hbm.1) | copy-start | bytes 49156

commit v2 on v0

v2 whole, which is shorter than its diff:
```python
import jax
import jax.numpy as jnp
from jax import lax
from jax.experimental import pallas as pl
from jax.experimental.pallas import tpu as pltpu
from jax.sharding import PartitionSpec as P

MESH = pl.DeviceIdType.MESH
F32, BF16 = jnp.float32, jnp.bfloat16
ITERS = 3
USERS, RANK, WEEKS, ITEMS = 128, 64, 64, 256
HALF, CHUNK, BLOCK = 64, 32, 16
CHUNKS, BLOCKS = HALF // CHUNK, CHUNK // BLOCK
PACK = CHUNK // 2
X, Y, Z = 4, 4, 8
FULL = X * Y


def by_distance(offsets, sizes):
    far = lambda o: sum(min(d, n - d) for d, n in zip(o, sizes))
    return sorted(offsets, key=far, reverse=True)


PLANE = by_distance([(dx, dy) for dx in range(X) for dy in range(Y)], (X, Y))
RING = by_distance([(dz,) for dz in range(Z)], (Z,))


def rows_of(step, chunk):
    return PACK + 8 if step == 0 and chunk == 0 else PACK


def kernel(
    counts_hbm, user_hbm, item_hbm, week_hbm, out_ref,
    counts, user_turned, user, items, week, pair_week, model_rhs, phi_rhs, models, factor, phi, held,
    half_src, half_dst, plane, ring,
    load_sem, count_sem, item_sems, swap_send, swap_recv, held_send, held_recv,
    half_send, half_recv, plane_send, plane_recv, ring_send, ring_recv,
):
    item, z_hi = lax.axis_index("item"), lax.axis_index("week")
    core, flat = lax.rem(item, 2), lax.rem(item // 2, FULL)
    x, y = lax.rem(flat, X), flat // X
    z = z_hi * 2 + item // (2 * FULL)

    def on(c):
        return pl.when(core == c)

    def in_plane(c, dx, dy):
        there = lax.rem(y + dy, Y) * X + lax.rem(x + dx, X)
        return {"item": item - core + c + (there - flat) * 2, "week": z_hi}

    def in_ring(c, dz):
        there = lax.rem(z + dz, Z)
        return {"item": lax.rem(there, 2) * (2 * FULL) + flat * 2 + c, "week": there // 2}

    other = in_ring(1 - core, 0)
    plane_peers = [[in_plane(c, *o) for o in PLANE] for c in range(2)]
    ring_peers = [[in_ring(c, *o) for o in RING] for c in range(2)]

    barrier = pltpu.get_barrier_semaphore()

    def greet(peers):
        for peer in peers:
            pl.semaphore_signal(barrier, inc=1, device_id=peer, device_id_type=MESH)

    @on(0)
    def _():
        greet(ring_peers[1])

    @on(1)
    def _():
        greet(plane_peers[0][:-1] + plane_peers[1][:-1] + ring_peers[1][:-1] + plane_peers[0][-1:])

    def remote(src, dst, send, recv, peer):
        return pltpu.make_async_remote_copy(
            src_ref=src, dst_ref=dst, send_sem=send, recv_sem=recv, device_id=peer, device_id_type=MESH
        )

    loads = [
        pltpu.make_async_copy(src, dst, load_sem.at[i])
        for i, (src, dst) in enumerate(((item_hbm, items.at[0]), (week_hbm, week), (user_hbm, user_turned)))
    ]
    for load in loads:
        load.start()
    first_blocks = [
        (chunk, half, b * BLOCK) for chunk in range(CHUNKS) for half in range(2) for b in range(BLOCKS)
    ]
    count_loads = []
    for i, (chunk, half, row) in enumerate(first_blocks):
        at = pl.ds(half * HALF + chunk * CHUNK + row, BLOCK)
        load = pltpu.make_async_copy(counts_hbm.at[at], counts.at[at], count_sem.at[i])
        load.start()
        count_loads.append(load)
    for load in loads:
        load.wait()

    left = lax.broadcasted_iota(jnp.int32, (1, 2 * RANK), 1) < RANK
    low_lanes = jnp.where(left, 0.0, 1.0).astype(F32)

    def build_rhs(which):
        values = items[which]
        high = values.astype(BF16).astype(F32)
        low = values - high
        model_rhs[which] = jnp.concatenate([high, high, low, low], axis=0).astype(BF16)
        both = jnp.concatenate([high, low], axis=0).T
        phi_rhs[which] = both.astype(BF16)
        sums = jnp.sum(both, axis=0, keepdims=True)
        return sums + pltpu.roll(sums, RANK, 1)

    item_sums = build_rhs(0)
    weeks = week[...]
    pair_week[...] = jnp.concatenate([weeks, weeks], axis=1)
    share = jnp.broadcast_to(item_sums * jnp.sum(pair_week[...], axis=0, keepdims=True), (8, 2 * RANK))
    user[...] = user_turned[...].T

    for half in range(2):
        for chunk in range(CHUNKS):
            rows = user[half * HALF + chunk * CHUNK : half * HALF + (chunk + 1) * CHUNK, :]
            factor[half, chunk] = jnp.concatenate([rows, rows], axis=1)
            held[half, chunk] = jnp.concatenate([rows[:PACK], rows[PACK:]], axis=1)

    def model(block):
        _, half, chunk, row, which, _, _ = block
        w = pair_week[...]
        parts = []
        for u in range(BLOCK):
            scaled = factor[half, chunk, row + u : row + u + 1, :] * w
            high = scaled.astype(BF16).astype(F32)
            parts.append((scaled - high * low_lanes).astype(BF16))
        lhs = jnp.concatenate(parts, axis=0)
        return jnp.dot(jnp.concatenate([lhs, lhs], axis=1), model_rhs[which], preferred_element_type=F32)

    def accumulate(block, slot):
        start, _, _, row, which, into, add = block
        c = counts[pl.ds(start, BLOCK)].reshape(BLOCK * WEEKS, ITEMS).astype(F32)
        ratio = c * pl.reciprocal(models[slot], approx=False)
        high = ratio.astype(BF16)
        low = (ratio - high.astype(F32)).astype(BF16)
        rhs = phi_rhs[which]
        sums = jnp.dot(high, rhs, preferred_element_type=F32) + jnp.dot(low, rhs, preferred_element_type=F32)
        sums = jnp.sum(sums.reshape(BLOCK, WEEKS, 2 * RANK) * pair_week[...][None], axis=1)
        if add:
            sums = sums + phi[into, row : row + BLOCK, :]
        phi[into, row : row + BLOCK, :] = sums

    def pack(half):
        both = phi[half]
        both = both + pltpu.roll(both, RANK, 1)
        return jnp.where(left, both[:PACK], both[PACK:])

    def compute(blocks, before, after):
        before(0)
        models[0] = model(blocks[0])
        for j, block in enumerate(blocks):
            if j + 1 < len(blocks):
                coming = model(blocks[j + 1])
                before(j + 1)
            accumulate(block, j % 2)
            if j + 1 < len(blocks):
                models[(j + 1) % 2] = coming
            after(j)

    def wait_bytes(ref, sem):
        pltpu.make_async_copy(ref, ref, sem).wait()

    def total(parts):
        while len(parts) > 1:
            parts = [a + b for a, b in zip(parts[::2], parts[1::2])]
        return parts[0]

    def share_half(chunk, half):
        n = rows_of(0, chunk)
        mine = pack(half)
        half_src[chunk, half, :PACK] = mine
        if n > PACK:
            half_src[chunk, half, PACK:n] = share

        @on(0)
        def _():
            at = pl.ds(0, n)
            remote(
                half_src.at[chunk, half, at], half_dst.at[chunk, half, at],
                half_send.at[chunk, half], half_recv.at[chunk, half], other,
            ).start()

    def send_first(chunk, half):
        n = rows_of(0, chunk)

        @on(1)
        def _():
            wait_bytes(half_dst.at[chunk, half, pl.ds(0, n)], half_recv.at[chunk, half])
            plane[0, chunk, half, flat, :n] = half_src[chunk, half, :n] + half_dst[chunk, half, :n]
            block = plane.at[0, chunk, half, flat, pl.ds(0, n)]
            for peer in plane_peers[1][:-1]:
                remote(block, block, plane_send.at[0, chunk, half], plane_recv.at[0, chunk, half], peer).start()

    def send_plane(step, chunk):
        plane[step, chunk, core, flat, :PACK] = pack(0)
        for c, peers in ((0, plane_peers[1]), (1, plane_peers[1][:-1])):

            @on(c)
            def _():
                block = plane.at[step, chunk, c, flat, pl.ds(0, PACK)]
                for peer in peers:
                    remote(block, block, plane_send.at[step, chunk, c], plane_recv.at[step, chunk, c], peer).start()

    def ring_targets(step, half):
        last = step == ITERS - 1
        return (ring_peers[0] if last or half == 0 else []) + (ring_peers[1][:-1] if last or half == 1 else [])

    def send_ring(step, chunk, half):
        n = rows_of(step, chunk)

        @on(1)
        def _():
            arriving = FULL if step and half == 0 else FULL - 1
            wait_bytes(plane.at[step, chunk, half, pl.ds(0, arriving), pl.ds(0, n)], plane_recv.at[step, chunk, half])
            ring[step, chunk, half, z, :n] = total([plane[step, chunk, half, j, :n] for j in range(FULL)])
            block = ring.at[step, chunk, half, z, pl.ds(0, n)]
            for peer in ring_targets(step, half):
                remote(block, block, ring_send.at[step, chunk, half], ring_recv.at[step, chunk, half], peer).start()

    def wait_ring(step, chunk, c, half):
        at = pl.ds(0, Z - c), pl.ds(0, rows_of(step, chunk))
        wait_bytes(ring.at[(step, chunk, half, *at)], ring_recv.at[step, chunk, half])

    denominator = {}

    def update(step, chunk):
        n = rows_of(step, chunk)
        for c in range(2):

            @on(c)
            def _():
                wait_ring(step, chunk, c, c)

        sums = total([ring[step, chunk, core, j, :n] for j in range(Z)])
        if n > PACK:
            denominator[0] = sums[PACK : PACK + 1]
        new = held[core, chunk] * sums[:PACK] / denominator[0]
        held[core, chunk] = new
        turned = pltpu.roll(new, RANK, 1)
        factor[core, chunk, :PACK] = jnp.where(left, new, turned)
        factor[core, chunk, PACK:] = jnp.where(left, turned, new)
        if step == ITERS - 2:
            mine = held.at[core, chunk]
            remote(mine, mine, held_send.at[chunk], held_recv.at[chunk], other).start()

    def before_first(j):
        count_loads[j].wait()

    def after_first(j):
        chunk, half, row = first_blocks[j]
        if row + BLOCK < CHUNK:
            return
        if chunk == 0 and half == 0:
            for c, n in ((0, FULL), (1, FULL - 1 + Z - 1 + Z)):

                @on(c)
                def _():
                    pl.semaphore_wait(barrier, n)

            remote(items.at[0], items.at[1], item_sems.at[0], item_sems.at[1], other).start()
        share_half(chunk, half)
        if half:
            send_first(chunk, 0)
        elif chunk:
            send_first(chunk - 1, 1)

    blocks = [
        (half * HALF + chunk * CHUNK + row, half, chunk, row, 0, half, False) for chunk, half, row in first_blocks
    ]
    compute(blocks, before_first, after_first)
    swaps = []
    for chunk in range(CHUNKS):
        theirs = pl.ds(pl.multiple_of((1 - core) * HALF + chunk * CHUNK, CHUNK), CHUNK)
        landing = pl.ds(USERS + chunk * CHUNK, CHUNK)
        swap = remote(counts_hbm.at[theirs], counts.at[landing], swap_send.at[chunk], swap_recv.at[chunk], other)
        swap.start()
        swaps.append(swap)
    wait_bytes(items.at[1], item_sems.at[1])
    build_rhs(1)
    send_first(CHUNKS - 1, 1)
    for chunk in range(CHUNKS):
        for half in range(2):
            send_ring(0, chunk, half)

    def later(chunk):
        own = pl.multiple_of(core * HALF + chunk * CHUNK, CHUNK)
        blocks = [
            (start + row, core, chunk, row, which, 0, which > 0)
            for which, start in enumerate((own, USERS + chunk * CHUNK))
            for row in range(0, CHUNK, BLOCK)
        ]
        compute(blocks, lambda j: None, lambda j: None)

    for step in range(1, ITERS):
        for chunk in range(CHUNKS):
            update(step - 1, chunk)
            if step == 1:
                swaps[chunk].wait_recv()
            later(chunk)
            send_plane(step, chunk)
        for chunk in range(CHUNKS):
            send_ring(step, chunk, 1)
            send_ring(step, chunk, 0)

    for chunk in range(CHUNKS):
        wait_bytes(held.at[0, chunk], held_recv.at[chunk])
        for half in (1, 0):
            for c in range(2):

                @on(c)
                def _():
                    wait_ring(ITERS - 1, chunk, c, half)

            sums = total([ring[ITERS - 1, chunk, half, j, :PACK] for j in range(Z)])
            new = held[half, chunk] * sums / denominator[0]
            at = half * HALF + chunk * CHUNK
            user[at : at + PACK, :] = new[:, :RANK]
            user[at + PACK : at + CHUNK, :] = new[:, RANK:]
    out_ref[...] = user[...].T

    wait_bytes(items.at[0], item_sems.at[0])
    for chunk in range(CHUNKS):
        swaps[chunk].wait_send()
        wait_bytes(held.at[0, chunk], held_send.at[chunk])

    def wait_sent(step, chunk, half, blocks, sem):
        if blocks:
            at = pl.ds(0, blocks), pl.ds(0, rows_of(step, chunk))
            wait_bytes(plane.at[(step, chunk, half, *at)], sem.at[step, chunk, half])

    @on(0)
    def _():
        for chunk in range(CHUNKS):
            for half in range(2):
                wait_bytes(half_src.at[chunk, half, pl.ds(0, rows_of(0, chunk))], half_send.at[chunk, half])
            for step in range(1, ITERS):
                wait_sent(step, chunk, 0, FULL, plane_send)

    @on(1)
    def _():
        for chunk in range(CHUNKS):
            for step in range(ITERS):
                for half in range(2):
                    wait_sent(step, chunk, half, FULL - 1 if half or not step else 0, plane_send)
                    wait_sent(step, chunk, half, len(ring_targets(step, half)), ring_send)


def per_device(counts, user_factor, item_factor, week_factor):
    most = PACK + 8
    dma = pltpu.SemaphoreType.DMA
    each = (ITERS, CHUNKS, 2)
    arrays = counts, user_factor.T, item_factor.T, week_factor
    turned = pl.pallas_call(
        kernel,
        out_shape=pltpu.VMEM((RANK, USERS), F32),
        in_specs=[pl.BlockSpec(memory_space=pltpu.HBM)] * 4,
        out_specs=pl.BlockSpec(memory_space=pltpu.VMEM),
        scratch_shapes=[
            pltpu.VMEM((USERS + HALF, WEEKS, ITEMS), jnp.int32),
            pltpu.VMEM((RANK, USERS), F32),
            pltpu.VMEM((USERS, RANK), F32),
            pltpu.VMEM((2, RANK, ITEMS), F32),
            pltpu.VMEM((WEEKS, RANK), F32),
            pltpu.VMEM((WEEKS, 2 * RANK), F32),
            pltpu.VMEM((2, 4 * RANK, ITEMS), BF16),
            pltpu.VMEM((2, ITEMS, 2 * RANK), BF16),
            pltpu.VMEM((2, BLOCK * WEEKS, ITEMS), F32),
            pltpu.VMEM((2, CHUNKS, CHUNK, 2 * RANK), F32),
            pltpu.VMEM((2, CHUNK, 2 * RANK), F32),
            pltpu.VMEM((2, CHUNKS, PACK, 2 * RANK), F32),
            pltpu.VMEM((CHUNKS, 2, most, 2 * RANK), F32),
            pltpu.VMEM((CHUNKS, 2, most, 2 * RANK), F32),
            pltpu.VMEM((*each, FULL, most, 2 * RANK), F32),
            pltpu.VMEM((*each, Z, most, 2 * RANK), F32),
            dma((3,)), dma((len(range(0, USERS, BLOCK)),)), dma((2,)), dma((CHUNKS,)), dma((CHUNKS,)),
            dma((CHUNKS,)), dma((CHUNKS,)), dma((CHUNKS, 2)), dma((CHUNKS, 2)),
            dma(each), dma(each), dma(each), dma(each),
        ],
        compiler_params=pltpu.CompilerParams(
            collective_id=0, has_side_effects=True, vmem_limit_bytes=48 << 20
        ),
        name="updates",
    )(*[pltpu.with_memory_space_constraint(a, pltpu.HBM) for a in arrays])
    return turned.T


def solution(mesh):
    placed = (P(None, "week", "item"), P(), P("item", None), P("week", None))
    return jax.shard_map(per_device, mesh=mesh, in_specs=placed, out_specs=P(), check_vma=False)
```

time: 474 us -> 51.2 us (0.11); the launches traced: 467 us -> 51.1 us
  blocking collectives: 379 us -> 0 us
  matrix products: 67 us -> 0 us
  Pallas kernels: 0 us -> 50.5 us
  local copies, waits for them, and re-layouts: 12.1 us -> 0.62 us
  other arithmetic: 8.19 us -> 0 us
    psum x5 -> x0, blocking collectives: 379 us -> none  [the longest x3 227 us: combine(): return lax.psum(partials, ('item', 'week'))]
    dot_general x6 -> x0, matrix products: 67 us -> none  [the longest x3 50.3 us: per_device(): model = jnp.dot(factor, khatri_rao.T, precision=lax.Precision.HIGHEST)]
    pallas_call x0 -> x1, Pallas kernels: none -> 50.5 us  [per_device(): pl.pallas_call(kernel, out_shape=pltpu.VMEM((RANK, USERS), F32), in_specs...]
    convert_element_type x1 -> x0, local copies, waits for them, and re-layouts: 9.24 us -> none  [per_device(): ratio = flat_counts.astype(jnp.float32) / model]
where the time goes in v2:
time: 51.2 us; the launch traced here: 51.1 us
  Pallas kernels  50.5 us (99%)
  local copies, waits for them, and re-layouts  0.62 us (1%)
    pallas_call x1, Pallas kernels, per_device(): pl.pallas_call(kernel, out_shape=pltpu.VMEM((RANK, USERS), F32), in_specs...  50.5 us

profile of v2, /device:TPU:1, one launch (start us, length us, event | category | flops | bytes accessed | tf_op | source)
XLA Modules:
  0.0 51.1 jit_solution(14358455874389169074)
XLA Ops:
  0.0 50.5 %updates.1 = f32[64,128]{1,0:T(8,128)S(1)} custom-call(s32[128,64,256]{2,1,0:T(8,128)} %counts_hbm.1, f32[64,128]{1,0:T(8,128)} %bitcast.5, f32[64,256]{1,0:T(8,128)} %bitcast.4, f32[64,64]{1,0:T(8,128)} %week_hbm.1), custom_call_target="tpu_custom_call" | custom-call | tf_op jit(solution)/shard_map/updates/pallas_call | solution.py:355
  50.5 0.6 %copy.6 = f32[128,64]{0,1:T(8,128)} copy(f32[128,64]{0,1:T(8,128)S(1)} %bitcast.3) | data formatting | bytes 65536

commit v3 on v2

--- a/solution.py
+++ b/solution.py
@@ -31,9 +31,9 @@
 
 def kernel(
     counts_hbm, user_hbm, item_hbm, week_hbm, out_ref,
-    counts, user_turned, user, items, week, pair_week, model_rhs, phi_rhs, models, factor, phi, held,
+    counts, user_turned, user, items, week, pair_week, model_rhs, phi_rhs, models, factor, phi, held, final,
     half_src, half_dst, plane, ring,
-    load_sem, count_sem, item_sems, swap_send, swap_recv, held_send, held_recv,
+    load_sem, count_sem, item_sems, swap_send, swap_recv, held_send, held_recv, final_send, final_recv,
     half_send, half_recv, plane_send, plane_recv, ring_send, ring_recv,
 ):
     item, z_hi = lax.axis_index("item"), lax.axis_index("week")
@@ -56,20 +56,6 @@
     plane_peers = [[in_plane(c, *o) for o in PLANE] for c in range(2)]
     ring_peers = [[in_ring(c, *o) for o in RING] for c in range(2)]
 
-    barrier = pltpu.get_barrier_semaphore()
-
-    def greet(peers):
-        for peer in peers:
-            pl.semaphore_signal(barrier, inc=1, device_id=peer, device_id_type=MESH)
-
-    @on(0)
-    def _():
-        greet(ring_peers[1])
-
-    @on(1)
-    def _():
-        greet(plane_peers[0][:-1] + plane_peers[1][:-1] + ring_peers[1][:-1] + plane_peers[0][-1:])
-
     def remote(src, dst, send, recv, peer):
         return pltpu.make_async_remote_copy(
             src_ref=src, dst_ref=dst, send_sem=send, recv_sem=recv, device_id=peer, device_id_type=MESH
@@ -81,6 +67,20 @@
     ]
     for load in loads:
         load.start()
+    barrier = pltpu.get_barrier_semaphore()
+
+    def greet(peers):
+        for peer in peers:
+            pl.semaphore_signal(barrier, inc=1, device_id=peer, device_id_type=MESH)
+
+    @on(0)
+    def _():
+        greet(ring_peers[1])
+
+    @on(1)
+    def _():
+        greet(plane_peers[1][:-1] + ring_peers[1][:-1] + [other])
+
     first_blocks = [
         (chunk, half, b * BLOCK) for chunk in range(CHUNKS) for half in range(2) for b in range(BLOCKS)
     ]
@@ -204,8 +204,7 @@
                     remote(block, block, plane_send.at[step, chunk, c], plane_recv.at[step, chunk, c], peer).start()
 
     def ring_targets(step, half):
-        last = step == ITERS - 1
-        return (ring_peers[0] if last or half == 0 else []) + (ring_peers[1][:-1] if last or half == 1 else [])
+        return ring_peers[0] if half == 0 and step < ITERS - 1 else ring_peers[1][:-1]
 
     def send_ring(step, chunk, half):
         n = rows_of(step, chunk)
@@ -242,8 +241,12 @@
         factor[core, chunk, :PACK] = jnp.where(left, new, turned)
         factor[core, chunk, PACK:] = jnp.where(left, turned, new)
         if step == ITERS - 2:
-            mine = held.at[core, chunk]
-            remote(mine, mine, held_send.at[chunk], held_recv.at[chunk], other).start()
+
+            @on(0)
+            def _():
+                mine = held.at[0, chunk]
+                remote(mine, mine, held_send.at[chunk], held_recv.at[chunk], other).start()
+
 
     def before_first(j):
         count_loads[j].wait()
@@ -253,13 +256,12 @@
         if row + BLOCK < CHUNK:
             return
         if chunk == 0 and half == 0:
-            for c, n in ((0, FULL), (1, FULL - 1 + Z - 1 + Z)):
+            for c, n in ((0, 1), (1, FULL - 1 + Z - 1 + Z)):
 
                 @on(c)
                 def _():
                     pl.semaphore_wait(barrier, n)
 
-            remote(items.at[0], items.at[1], item_sems.at[0], item_sems.at[1], other).start()
         share_half(chunk, half)
         if half:
             send_first(chunk, 0)
@@ -270,6 +272,7 @@
         (half * HALF + chunk * CHUNK + row, half, chunk, row, 0, half, False) for chunk, half, row in first_blocks
     ]
     compute(blocks, before_first, after_first)
+    remote(items.at[0], items.at[1], item_sems.at[0], item_sems.at[1], other).start()
     swaps = []
     for chunk in range(CHUNKS):
         theirs = pl.ds(pl.multiple_of((1 - core) * HALF + chunk * CHUNK, CHUNK), CHUNK)
@@ -304,17 +307,26 @@
             send_ring(step, chunk, 1)
             send_ring(step, chunk, 0)
 
+    @on(1)
+    def _():
+        for chunk in range(CHUNKS):
+            wait_bytes(held.at[0, chunk], held_recv.at[chunk])
+            for half in (1, 0):
+                wait_ring(ITERS - 1, chunk, 1, half)
+                sums = total([ring[ITERS - 1, chunk, half, j, :PACK] for j in range(Z)])
+                final[half, chunk] = held[half, chunk] * sums / denominator[0]
+                mine = final.at[half, chunk]
+                remote(mine, mine, final_send.at[chunk, half], final_recv.at[chunk, half], other).start()
+
+    @on(0)
+    def _():
+        for chunk in range(CHUNKS):
+            for half in (1, 0):
+                wait_bytes(final.at[half, chunk], final_recv.at[chunk, half])
+
     for chunk in range(CHUNKS):
-        wait_bytes(held.at[0, chunk], held_recv.at[chunk])
-        for half in (1, 0):
-            for c in range(2):
-
-                @on(c)
-                def _():
-                    wait_ring(ITERS - 1, chunk, c, half)
-
-            sums = total([ring[ITERS - 1, chunk, half, j, :PACK] for j in range(Z)])
-            new = held[half, chunk] * sums / denominator[0]
+        for half in range(2):
+            new = final[half, chunk]
             at = half * HALF + chunk * CHUNK
             user[at : at + PACK, :] = new[:, :RANK]
             user[at + PACK : at + CHUNK, :] = new[:, RANK:]
@@ -323,7 +335,6 @@
     wait_bytes(items.at[0], item_sems.at[0])
     for chunk in range(CHUNKS):
         swaps[chunk].wait_send()
-        wait_bytes(held.at[0, chunk], held_send.at[chunk])
 
     def wait_sent(step, chunk, half, blocks, sem):
         if blocks:
@@ -333,6 +344,7 @@
     @on(0)
     def _():
         for chunk in range(CHUNKS):
+            wait_bytes(held.at[0, chunk], held_send.at[chunk])
             for half in range(2):
                 wait_bytes(half_src.at[chunk, half, pl.ds(0, rows_of(0, chunk))], half_send.at[chunk, half])
             for step in range(1, ITERS):
@@ -341,6 +353,8 @@
     @on(1)
     def _():
         for chunk in range(CHUNKS):
+            for half in range(2):
+                wait_bytes(final.at[half, chunk], final_send.at[chunk, half])
             for step in range(ITERS):
                 for half in range(2):
                     wait_sent(step, chunk, half, FULL - 1 if half or not step else 0, plane_send)
@@ -370,12 +384,13 @@
             pltpu.VMEM((2, CHUNKS, CHUNK, 2 * RANK), F32),
             pltpu.VMEM((2, CHUNK, 2 * RANK), F32),
             pltpu.VMEM((2, CHUNKS, PACK, 2 * RANK), F32),
+            pltpu.VMEM((2, CHUNKS, PACK, 2 * RANK), F32),
             pltpu.VMEM((CHUNKS, 2, most, 2 * RANK), F32),
             pltpu.VMEM((CHUNKS, 2, most, 2 * RANK), F32),
             pltpu.VMEM((*each, FULL, most, 2 * RANK), F32),
             pltpu.VMEM((*each, Z, most, 2 * RANK), F32),
             dma((3,)), dma((len(range(0, USERS, BLOCK)),)), dma((2,)), dma((CHUNKS,)), dma((CHUNKS,)),
-            dma((CHUNKS,)), dma((CHUNKS,)), dma((CHUNKS, 2)), dma((CHUNKS, 2)),
+            dma((CHUNKS,)), dma((CHUNKS,)), dma((CHUNKS, 2)), dma((CHUNKS, 2)), dma((CHUNKS, 2)), dma((CHUNKS, 2)),
             dma(each), dma(each), dma(each), dma(each),
         ],
         compiler_params=pltpu.CompilerParams(

time: 51.2 us -> 48.6 us (0.949)
  Pallas kernels: 50.5 us -> 47.9 us
    pallas_call x1, Pallas kernels: 50.5 us -> 47.9 us  [per_device(): pl.pallas_call(kernel, out_shape=pltpu.VMEM((RANK, USERS), F32), in_specs...]
where the time goes in v3:
time: 48.6 us; the launch traced here: 48.5 us
  Pallas kernels  47.9 us (99%)
  local copies, waits for them, and re-layouts  0.62 us (1%)
    pallas_call x1, Pallas kernels, per_device(): pl.pallas_call(kernel, out_shape=pltpu.VMEM((RANK, USERS), F32), in_specs...  47.9 us

profile of v3, /device:TPU:1, one launch (start us, length us, event | category | flops | bytes accessed | tf_op | source)
XLA Modules:
  0.0 48.5 jit_solution(10832789121695622488)
XLA Ops:
  0.0 47.9 %updates.1 = f32[64,128]{1,0:T(8,128)S(1)} custom-call(s32[128,64,256]{2,1,0:T(8,128)} %counts_hbm.1, f32[64,128]{1,0:T(8,128)} %bitcast.5, f32[64,256]{1,0:T(8,128)} %bitcast.4, f32[64,64]{1,0:T(8,128)} %week_hbm.1), custom_call_target="tpu_custom_call" | custom-call | tf_op jit(solution)/shard_map/updates/pallas_call | solution.py:369
  47.9 0.6 %copy.6 = f32[128,64]{0,1:T(8,128)} copy(f32[128,64]{0,1:T(8,128)S(1)} %bitcast.3) | data formatting | bytes 65536

commit v4 on v3

--- a/solution.py
+++ b/solution.py
@@ -31,7 +31,7 @@
 
 def kernel(
     counts_hbm, user_hbm, item_hbm, week_hbm, out_ref,
-    counts, user_turned, user, items, week, pair_week, model_rhs, phi_rhs, models, factor, phi, held, final,
+    raw_counts, counts, user_turned, user, items, week, pair_week, model_rhs, phi_rhs, models, factor, phi, held, final,
     half_src, half_dst, plane, ring,
     load_sem, count_sem, item_sems, swap_send, swap_recv, held_send, held_recv, final_send, final_recv,
     half_send, half_recv, plane_send, plane_recv, ring_send, ring_recv,
@@ -87,20 +87,19 @@
     count_loads = []
     for i, (chunk, half, row) in enumerate(first_blocks):
         at = pl.ds(half * HALF + chunk * CHUNK + row, BLOCK)
-        load = pltpu.make_async_copy(counts_hbm.at[at], counts.at[at], count_sem.at[i])
+        load = pltpu.make_async_copy(counts_hbm.at[at], raw_counts.at[at], count_sem.at[i])
         load.start()
         count_loads.append(load)
     for load in loads:
         load.wait()
 
     left = lax.broadcasted_iota(jnp.int32, (1, 2 * RANK), 1) < RANK
-    low_lanes = jnp.where(left, 0.0, 1.0).astype(F32)
 
     def build_rhs(which):
         values = items[which]
         high = values.astype(BF16).astype(F32)
         low = values - high
-        model_rhs[which] = jnp.concatenate([high, high, low, low], axis=0).astype(BF16)
+        model_rhs[which] = jnp.concatenate([high, low, high, low], axis=0).astype(BF16)
         both = jnp.concatenate([high, low], axis=0).T
         phi_rhs[which] = both.astype(BF16)
         sums = jnp.sum(both, axis=0, keepdims=True)
@@ -121,24 +120,34 @@
     def model(block):
         _, half, chunk, row, which, _, _ = block
         w = pair_week[...]
-        parts = []
+        highs, lows = [], []
         for u in range(BLOCK):
             scaled = factor[half, chunk, row + u : row + u + 1, :] * w
-            high = scaled.astype(BF16).astype(F32)
-            parts.append((scaled - high * low_lanes).astype(BF16))
-        lhs = jnp.concatenate(parts, axis=0)
-        return jnp.dot(jnp.concatenate([lhs, lhs], axis=1), model_rhs[which], preferred_element_type=F32)
+            high = scaled.astype(BF16)
+            highs.append(high)
+            lows.append((scaled - high.astype(F32)).astype(BF16))
+        lhs = jnp.concatenate([jnp.concatenate(highs, axis=0), jnp.concatenate(lows, axis=0)], axis=1)
+        return jnp.dot(lhs, model_rhs[which], preferred_element_type=F32)
 
     def accumulate(block, slot):
-        start, _, _, row, which, into, add = block
-        c = counts[pl.ds(start, BLOCK)].reshape(BLOCK * WEEKS, ITEMS).astype(F32)
+        start, _, _, row, which, into, later_on = block
+        if later_on is None:
+            c = raw_counts[pl.ds(start, BLOCK)].astype(F32)
+            counts[pl.ds(start, BLOCK)] = c
+        else:
+            c = counts[pl.ds(start, BLOCK)]
+        c = c.reshape(BLOCK * WEEKS, ITEMS)
         ratio = c * pl.reciprocal(models[slot], approx=False)
         high = ratio.astype(BF16)
         low = (ratio - high.astype(F32)).astype(BF16)
         rhs = phi_rhs[which]
-        sums = jnp.dot(high, rhs, preferred_element_type=F32) + jnp.dot(low, rhs, preferred_element_type=F32)
+        sums = jnp.dot(
+            jnp.concatenate([high, low], axis=1),
+            jnp.concatenate([rhs, rhs], axis=0),
+            preferred_element_type=F32,
+        )
         sums = jnp.sum(sums.reshape(BLOCK, WEEKS, 2 * RANK) * pair_week[...][None], axis=1)
-        if add:
+        if later_on:
             sums = sums + phi[into, row : row + BLOCK, :]
         phi[into, row : row + BLOCK, :] = sums
 
@@ -148,12 +157,12 @@
         return jnp.where(left, both[:PACK], both[PACK:])
 
     def compute(blocks, before, after):
-        before(0)
-        models[0] = model(blocks[0])
         for j, block in enumerate(blocks):
+            before(j)
+            if j == 0:
+                models[0] = model(block)
             if j + 1 < len(blocks):
                 coming = model(blocks[j + 1])
-                before(j + 1)
             accumulate(block, j % 2)
             if j + 1 < len(blocks):
                 models[(j + 1) % 2] = coming
@@ -221,6 +230,27 @@
     def wait_ring(step, chunk, c, half):
         at = pl.ds(0, Z - c), pl.ds(0, rows_of(step, chunk))
         wait_bytes(ring.at[(step, chunk, half, *at)], ring_recv.at[step, chunk, half])
+
+    def wait_sent(step, chunk, half, blocks, sem):
+        at = pl.ds(0, blocks), pl.ds(0, rows_of(step, chunk))
+        wait_bytes(plane.at[(step, chunk, half, *at)], sem.at[step, chunk, half])
+
+    def done_sending(step, sem):
+        if step and sem is plane_send:
+
+            @on(0)
+            def _():
+                for chunk in range(CHUNKS):
+                    wait_sent(step, chunk, 0, FULL, sem)
+
+        @on(1)
+        def _():
+            for chunk in range(CHUNKS):
+                for half in range(2):
+                    if sem is ring_send:
+                        wait_sent(step, chunk, half, len(ring_targets(step, half)), sem)
+                    elif half or not step:
+                        wait_sent(step, chunk, half, FULL - 1, sem)
 
     denominator = {}
 
@@ -249,7 +279,9 @@
 
 
     def before_first(j):
-        count_loads[j].wait()
+        if j % BLOCKS == 0:
+            for load in count_loads[j : j + BLOCKS]:
+                load.wait()
 
     def after_first(j):
         chunk, half, row = first_blocks[j]
@@ -269,7 +301,7 @@
             send_first(chunk - 1, 1)
 
     blocks = [
-        (half * HALF + chunk * CHUNK + row, half, chunk, row, 0, half, False) for chunk, half, row in first_blocks
+        (half * HALF + chunk * CHUNK + row, half, chunk, row, 0, half, None) for chunk, half, row in first_blocks
     ]
     compute(blocks, before_first, after_first)
     remote(items.at[0], items.at[1], item_sems.at[0], item_sems.at[1], other).start()
@@ -277,7 +309,7 @@
     for chunk in range(CHUNKS):
         theirs = pl.ds(pl.multiple_of((1 - core) * HALF + chunk * CHUNK, CHUNK), CHUNK)
         landing = pl.ds(USERS + chunk * CHUNK, CHUNK)
-        swap = remote(counts_hbm.at[theirs], counts.at[landing], swap_send.at[chunk], swap_recv.at[chunk], other)
+        swap = remote(counts.at[theirs], counts.at[landing], swap_send.at[chunk], swap_recv.at[chunk], other)
         swap.start()
         swaps.append(swap)
     wait_bytes(items.at[1], item_sems.at[1])
@@ -303,9 +335,30 @@
                 swaps[chunk].wait_recv()
             later(chunk)
             send_plane(step, chunk)
+        done_sending(step - 1, plane_send)
+        done_sending(step - 1, ring_send)
+        if step == 1:
+            wait_bytes(items.at[0], item_sems.at[0])
+            for swap in swaps:
+                swap.wait_send()
+
+            @on(0)
+            def _():
+                for chunk in range(CHUNKS):
+                    for half in range(2):
+                        wait_bytes(half_src.at[chunk, half, pl.ds(0, rows_of(0, chunk))], half_send.at[chunk, half])
+
+        if step == ITERS - 1:
+
+            @on(0)
+            def _():
+                for chunk in range(CHUNKS):
+                    wait_bytes(held.at[0, chunk], held_send.at[chunk])
+
         for chunk in range(CHUNKS):
             send_ring(step, chunk, 1)
             send_ring(step, chunk, 0)
+    done_sending(ITERS - 1, plane_send)
 
     @on(1)
     def _():
@@ -332,33 +385,13 @@
             user[at + PACK : at + CHUNK, :] = new[:, RANK:]
     out_ref[...] = user[...].T
 
-    wait_bytes(items.at[0], item_sems.at[0])
-    for chunk in range(CHUNKS):
-        swaps[chunk].wait_send()
-
-    def wait_sent(step, chunk, half, blocks, sem):
-        if blocks:
-            at = pl.ds(0, blocks), pl.ds(0, rows_of(step, chunk))
-            wait_bytes(plane.at[(step, chunk, half, *at)], sem.at[step, chunk, half])
-
-    @on(0)
-    def _():
-        for chunk in range(CHUNKS):
-            wait_bytes(held.at[0, chunk], held_send.at[chunk])
-            for half in range(2):
-                wait_bytes(half_src.at[chunk, half, pl.ds(0, rows_of(0, chunk))], half_send.at[chunk, half])
-            for step in range(1, ITERS):
-                wait_sent(step, chunk, 0, FULL, plane_send)
+    done_sending(ITERS - 1, ring_send)
 
     @on(1)
     def _():
         for chunk in range(CHUNKS):
             for half in range(2):
                 wait_bytes(final.at[half, chunk], final_send.at[chunk, half])
-            for step in range(ITERS):
-                for half in range(2):
-                    wait_sent(step, chunk, half, FULL - 1 if half or not step else 0, plane_send)
-                    wait_sent(step, chunk, half, len(ring_targets(step, half)), ring_send)
 
 
 def per_device(counts, user_factor, item_factor, week_factor):
@@ -372,7 +405,8 @@
         in_specs=[pl.BlockSpec(memory_space=pltpu.HBM)] * 4,
         out_specs=pl.BlockSpec(memory_space=pltpu.VMEM),
         scratch_shapes=[
-            pltpu.VMEM((USERS + HALF, WEEKS, ITEMS), jnp.int32),
+            pltpu.VMEM((USERS, WEEKS, ITEMS), jnp.int32),
+            pltpu.VMEM((USERS + HALF, WEEKS, ITEMS), F32),
             pltpu.VMEM((RANK, USERS), F32),
             pltpu.VMEM((USERS, RANK), F32),
             pltpu.VMEM((2, RANK, ITEMS), F32),

time: 48.6 us -> 47.1 us (0.969)
  Pallas kernels: 47.9 us -> 46.4 us
    pallas_call x1, Pallas kernels: 47.9 us -> 46.4 us  [per_device(): pl.pallas_call(kernel, out_shape=pltpu.VMEM((RANK, USERS), F32), in_specs...]
where the time goes in v4:
time: 47.1 us; the launch traced here: 47 us
  Pallas kernels  46.4 us (99%)
  local copies, waits for them, and re-layouts  0.62 us (1%)
    pallas_call x1, Pallas kernels, per_device(): pl.pallas_call(kernel, out_shape=pltpu.VMEM((RANK, USERS), F32), in_specs...  46.4 us

profile of v4, /device:TPU:1, one launch (start us, length us, event | category | flops | bytes accessed | tf_op | source)
XLA Modules:
  0.0 47.0 jit_solution(1146271145877813077)
XLA Ops:
  0.0 46.4 %updates.1 = f32[64,128]{1,0:T(8,128)S(1)} custom-call(s32[128,64,256]{2,1,0:T(8,128)} %counts_hbm.1, f32[64,128]{1,0:T(8,128)} %bitcast.5, f32[64,256]{1,0:T(8,128)} %bitcast.4, f32[64,64]{1,0:T(8,128)} %week_hbm.1), custom_call_target="tpu_custom_call" | custom-call | tf_op jit(solution)/shard_map/updates/pallas_call | solution.py:402
  46.4 0.6 %copy.6 = f32[128,64]{0,1:T(8,128)} copy(f32[128,64]{0,1:T(8,128)S(1)} %bitcast.3) | data formatting | bytes 65536

commit v5 on v4

--- a/solution.py
+++ b/solution.py
@@ -9,7 +9,7 @@
 F32, BF16 = jnp.float32, jnp.bfloat16
 ITERS = 3
 USERS, RANK, WEEKS, ITEMS = 128, 64, 64, 256
-HALF, CHUNK, BLOCK = 64, 32, 16
+HALF, CHUNK, BLOCK = 64, 32, 8
 CHUNKS, BLOCKS = HALF // CHUNK, CHUNK // BLOCK
 PACK = CHUNK // 2
 X, Y, Z = 4, 4, 8
@@ -270,13 +270,6 @@
         turned = pltpu.roll(new, RANK, 1)
         factor[core, chunk, :PACK] = jnp.where(left, new, turned)
         factor[core, chunk, PACK:] = jnp.where(left, turned, new)
-        if step == ITERS - 2:
-
-            @on(0)
-            def _():
-                mine = held.at[0, chunk]
-                remote(mine, mine, held_send.at[chunk], held_recv.at[chunk], other).start()
-
 
     def before_first(j):
         if j % BLOCKS == 0:
@@ -287,12 +280,11 @@
         chunk, half, row = first_blocks[j]
         if row + BLOCK < CHUNK:
             return
-        if chunk == 0 and half == 0:
-            for c, n in ((0, 1), (1, FULL - 1 + Z - 1 + Z)):
-
-                @on(c)
-                def _():
-                    pl.semaphore_wait(barrier, n)
+        if chunk == 0:
+
+            @on(half)
+            def _():
+                pl.semaphore_wait(barrier, (FULL - 1 + Z - 1 + Z) if half else 1)
 
         share_half(chunk, half)
         if half:
@@ -330,11 +322,18 @@
 
     for step in range(1, ITERS):
         for chunk in range(CHUNKS):
-            update(step - 1, chunk)
             if step == 1:
                 swaps[chunk].wait_recv()
+            update(step - 1, chunk)
             later(chunk)
             send_plane(step, chunk)
+            if step == ITERS - 1:
+
+                @on(0)
+                def _():
+                    mine = held.at[0, chunk]
+                    remote(mine, mine, held_send.at[chunk], held_recv.at[chunk], other).start()
+
         done_sending(step - 1, plane_send)
         done_sending(step - 1, ring_send)
         if step == 1:

time: 47.1 us -> 46.2 us (0.981)
  Pallas kernels: 46.4 us -> 45.5 us
    pallas_call x1, Pallas kernels: 46.4 us -> 45.5 us  [per_device(): pl.pallas_call(kernel, out_shape=pltpu.VMEM((RANK, USERS), F32), in_specs...]
where the time goes in v5:
time: 46.2 us; the launch traced here: 46.1 us
  Pallas kernels  45.5 us (98%)
  local copies, waits for them, and re-layouts  0.62 us (1%)
    pallas_call x1, Pallas kernels, per_device(): pl.pallas_call(kernel, out_shape=pltpu.VMEM((RANK, USERS), F32), in_specs...  45.5 us

profile of v5, /device:TPU:1, one launch (start us, length us, event | category | flops | bytes accessed | tf_op | source)
XLA Modules:
  0.0 46.1 jit_solution(1127636168023288274)
XLA Ops:
  0.0 45.5 %updates.1 = f32[64,128]{1,0:T(8,128)S(1)} custom-call(s32[128,64,256]{2,1,0:T(8,128)} %counts_hbm.1, f32[64,128]{1,0:T(8,128)} %bitcast.5, f32[64,256]{1,0:T(8,128)} %bitcast.4, f32[64,64]{1,0:T(8,128)} %week_hbm.1), custom_call_target="tpu_custom_call" | custom-call | tf_op jit(solution)/shard_map/updates/pallas_call | solution.py:401
  45.5 0.6 %copy.6 = f32[128,64]{0,1:T(8,128)} copy(f32[128,64]{0,1:T(8,128)S(1)} %bitcast.3) | data formatting | bytes 65536

commit v6 on v5

--- a/solution.py
+++ b/solution.py
@@ -212,7 +212,12 @@
                 for peer in peers:
                     remote(block, block, plane_send.at[step, chunk, c], plane_recv.at[step, chunk, c], peer).start()
 
-    def ring_targets(step, half):
+    def to_both(step, chunk, half):
+        return (step, chunk, half) == (ITERS - 1, CHUNKS - 1, 0)
+
+    def ring_targets(step, chunk, half):
+        if to_both(step, chunk, half):
+            return ring_peers[1][:-1] + ring_peers[0]
         return ring_peers[0] if half == 0 and step < ITERS - 1 else ring_peers[1][:-1]
 
     def send_ring(step, chunk, half):
@@ -224,7 +229,7 @@
             wait_bytes(plane.at[step, chunk, half, pl.ds(0, arriving), pl.ds(0, n)], plane_recv.at[step, chunk, half])
             ring[step, chunk, half, z, :n] = total([plane[step, chunk, half, j, :n] for j in range(FULL)])
             block = ring.at[step, chunk, half, z, pl.ds(0, n)]
-            for peer in ring_targets(step, half):
+            for peer in ring_targets(step, chunk, half):
                 remote(block, block, ring_send.at[step, chunk, half], ring_recv.at[step, chunk, half], peer).start()
 
     def wait_ring(step, chunk, c, half):
@@ -248,7 +253,7 @@
             for chunk in range(CHUNKS):
                 for half in range(2):
                     if sem is ring_send:
-                        wait_sent(step, chunk, half, len(ring_targets(step, half)), sem)
+                        wait_sent(step, chunk, half, len(ring_targets(step, chunk, half)), sem)
                     elif half or not step:
                         wait_sent(step, chunk, half, FULL - 1, sem)
 
@@ -359,21 +364,29 @@
             send_ring(step, chunk, 0)
     done_sending(ITERS - 1, plane_send)
 
+    def finish(c, chunk, half):
+        wait_ring(ITERS - 1, chunk, c, half)
+        sums = total([ring[ITERS - 1, chunk, half, j, :PACK] for j in range(Z)])
+        final[half, chunk] = held[half, chunk] * sums / denominator[0]
+
+    pieces = [(chunk, half) for chunk in range(CHUNKS) for half in (1, 0)]
+
     @on(1)
     def _():
-        for chunk in range(CHUNKS):
-            wait_bytes(held.at[0, chunk], held_recv.at[chunk])
-            for half in (1, 0):
-                wait_ring(ITERS - 1, chunk, 1, half)
-                sums = total([ring[ITERS - 1, chunk, half, j, :PACK] for j in range(Z)])
-                final[half, chunk] = held[half, chunk] * sums / denominator[0]
+        for chunk, half in pieces:
+            if half == 0:
+                wait_bytes(held.at[0, chunk], held_recv.at[chunk])
+            finish(1, chunk, half)
+            if not to_both(ITERS - 1, chunk, half):
                 mine = final.at[half, chunk]
                 remote(mine, mine, final_send.at[chunk, half], final_recv.at[chunk, half], other).start()
 
     @on(0)
     def _():
-        for chunk in range(CHUNKS):
-            for half in (1, 0):
+        for chunk, half in pieces:
+            if to_both(ITERS - 1, chunk, half):
+                finish(0, chunk, half)
+            else:
                 wait_bytes(final.at[half, chunk], final_recv.at[chunk, half])
 
     for chunk in range(CHUNKS):
@@ -388,8 +401,8 @@
 
     @on(1)
     def _():
-        for chunk in range(CHUNKS):
-            for half in range(2):
+        for chunk, half in pieces:
+            if not to_both(ITERS - 1, chunk, half):
                 wait_bytes(final.at[half, chunk], final_send.at[chunk, half])
 
 

time: 46.2 us -> 45.6 us (0.987)
  Pallas kernels: 45.5 us -> 44.9 us
    pallas_call x1, Pallas kernels: 45.5 us -> 44.9 us  [per_device(): pl.pallas_call(kernel, out_shape=pltpu.VMEM((RANK, USERS), F32), in_specs...]
where the time goes in v6:
time: 45.6 us; the launch traced here: 45.5 us
  Pallas kernels  44.9 us (98%)
  local copies, waits for them, and re-layouts  0.62 us (1%)
    pallas_call x1, Pallas kernels, per_device(): pl.pallas_call(kernel, out_shape=pltpu.VMEM((RANK, USERS), F32), in_specs...  44.9 us

profile of v6, /device:TPU:1, one launch (start us, length us, event | category | flops | bytes accessed | tf_op | source)
XLA Modules:
  0.0 45.5 jit_solution(342733349117967219)
XLA Ops:
  0.0 44.9 %updates.1 = f32[64,128]{1,0:T(8,128)S(1)} custom-call(s32[128,64,256]{2,1,0:T(8,128)} %counts_hbm.1, f32[64,128]{1,0:T(8,128)} %bitcast.5, f32[64,256]{1,0:T(8,128)} %bitcast.4, f32[64,64]{1,0:T(8,128)} %week_hbm.1), custom_call_target="tpu_custom_call" | custom-call | tf_op jit(solution)/shard_map/updates/pallas_call | solution.py:414
  44.9 0.6 %copy.6 = f32[128,64]{0,1:T(8,128)} copy(f32[128,64]{0,1:T(8,128)S(1)} %bitcast.3) | data formatting | bytes 65536

commit v7 on v6

--- a/solution.py
+++ b/solution.py
@@ -277,8 +277,10 @@
         factor[core, chunk, PACK:] = jnp.where(left, turned, new)
 
     def before_first(j):
-        if j % BLOCKS == 0:
-            for load in count_loads[j : j + BLOCKS]:
+        begin = 0 if j == 0 else BLOCKS // 2 if j == BLOCKS // 2 else j if j % BLOCKS == 0 else None
+        if begin is not None:
+            end = BLOCKS // 2 if j == 0 else BLOCKS if j == BLOCKS // 2 else j + BLOCKS
+            for load in count_loads[begin:end]:
                 load.wait()
 
     def after_first(j):
@@ -369,6 +371,12 @@
         sums = total([ring[ITERS - 1, chunk, half, j, :PACK] for j in range(Z)])
         final[half, chunk] = held[half, chunk] * sums / denominator[0]
 
+    def place(chunk, half):
+        new = final[half, chunk]
+        at = half * HALF + chunk * CHUNK
+        user[at : at + PACK, :] = new[:, :RANK]
+        user[at + PACK : at + CHUNK, :] = new[:, RANK:]
+
     pieces = [(chunk, half) for chunk in range(CHUNKS) for half in (1, 0)]
 
     @on(1)
@@ -380,6 +388,7 @@
             if not to_both(ITERS - 1, chunk, half):
                 mine = final.at[half, chunk]
                 remote(mine, mine, final_send.at[chunk, half], final_recv.at[chunk, half], other).start()
+                place(chunk, half)
 
     @on(0)
     def _():
@@ -388,13 +397,9 @@
                 finish(0, chunk, half)
             else:
                 wait_bytes(final.at[half, chunk], final_recv.at[chunk, half])
-
-    for chunk in range(CHUNKS):
-        for half in range(2):
-            new = final[half, chunk]
-            at = half * HALF + chunk * CHUNK
-            user[at : at + PACK, :] = new[:, :RANK]
-            user[at + PACK : at + CHUNK, :] = new[:, RANK:]
+                place(chunk, half)
+
+    place(*pieces[-1])
     out_ref[...] = user[...].T
 
     done_sending(ITERS - 1, ring_send)

time: 45.6 us -> 45.8 us (level)
  no operation moved by 1% of the time
where the time goes in v7:
time: 45.8 us; the launch traced here: 45.7 us
  Pallas kernels  45.1 us (98%)
  local copies, waits for them, and re-layouts  0.62 us (1%)
    pallas_call x1, Pallas kernels, per_device(): pl.pallas_call(kernel, out_shape=pltpu.VMEM((RANK, USERS), F32), in_specs...  45.1 us

profile of v7, /device:TPU:1, one launch (start us, length us, event | category | flops | bytes accessed | tf_op | source)
XLA Modules:
  0.0 45.7 jit_solution(8322924385377979311)
XLA Ops:
  0.0 45.1 %updates.1 = f32[64,128]{1,0:T(8,128)S(1)} custom-call(s32[128,64,256]{2,1,0:T(8,128)} %counts_hbm.1, f32[64,128]{1,0:T(8,128)} %bitcast.5, f32[64,256]{1,0:T(8,128)} %bitcast.4, f32[64,64]{1,0:T(8,128)} %week_hbm.1), custom_call_target="tpu_custom_call" | custom-call | tf_op jit(solution)/shard_map/updates/pallas_call | solution.py:419
  45.1 0.6 %copy.6 = f32[128,64]{0,1:T(8,128)} copy(f32[128,64]{0,1:T(8,128)S(1)} %bitcast.3) | data formatting | bytes 65536
